TPU v7x, 32 devices: a whole 2x2x4 slice. The times are simulated.
32 devices in a mesh: row: 4 (over y, x), col: 8 (over z, core).
Axes of the slice: x: 2, y: 2, z: 4, core: 2. Of those that a mesh axis runs over, the one named last changes fastest.
Arguments:
- ham_tiles: float32 [4, 8, 320, 128, 128], P('row', 'col'), may hold values from -0.0625 to 0.0625
- tile_list: int32 [4, 8, 320, 2], P('row', 'col'), may hold values from 0 to 31, as said below
- tile_count: int32 [4, 8], P('row', 'col'), may hold values from 1 to 320, as said below
- basis_block: float32 [16, 16384], P(None, ('row', 'col')), may hold values from -6 to 6
- residual_block: float32 [16, 16384], P(None, ('row', 'col')), may hold values from -6 to 6
Outputs:
- h_basis: float32 [16, 16384], P(None, ('row', 'col'))
- h_residual: float32 [16, 16384], P(None, ('row', 'col'))
Inputs may be any that keep to these rules, and one draw needn't show every extreme that they name: `tile_list`: entry 0 is a block row within the grid row, below 32; entry 1 a block column within the grid column, below 16. Live slots name distinct blocks with global row block at most the global column block; slots past the count name arbitrary blocks in range. `tile_count`: each device's count lies between half and all of its share of 320 in proportion to its upper-triangle slots, never above its distinct upper blocks; devices with the most upper-triangle slots hold exactly 320.
All inputs are finite; a program needn't handle non-finite values.
Results may differ from a plain program's by a relative error of at most 0.0003.
Values sent between devices are 32-bit elements; how exact they have to be, the bound alone decides.
No kernel may reach another device: no remote copies, remote signals or barrier semaphores. Data moves between devices by JAX's collectives and lax.ppermute only.
A program may use at most 128 MiB of HBM per device.

v0:
```python
import functools

import jax
import jax.numpy as jnp
from jax import lax
from jax.experimental import pallas as pl
from jax.experimental.pallas import tpu as pltpu
from jax.sharding import PartitionSpec as P

GROUP = 32
MIB = 1024 * 1024
VMEM = pl.BlockSpec(memory_space=pltpu.VMEM)
SMEM = pl.BlockSpec(memory_space=pltpu.SMEM)
ANY = pl.BlockSpec(memory_space=pl.ANY)


def small(kernel, out_shape, name, *args, in_specs=None):
    single = not isinstance(out_shape, list)
    return pl.pallas_call(
        kernel,
        out_shape=out_shape,
        in_specs=in_specs or [VMEM] * len(args),
        out_specs=VMEM if single else [VMEM] * len(out_shape),
        compiler_params=pltpu.CompilerParams(vmem_limit_bytes=2 * MIB),
        name=name,
    )(*args)


def f32(*shape):
    return jax.ShapeDtypeStruct(shape, jnp.float32)


def pass_kernel(in_ref, out_ref):
    out_ref[...] = in_ref[...]


def gather_kernel(*refs):
    *ins, out_ref = refs
    for q, ref in enumerate(reversed(ins)):
        out_ref[q] = ref[...]


def split(x):
    high = x.astype(jnp.bfloat16)
    low = (x - high.astype(jnp.float32)).astype(jnp.bfloat16)
    return high, low


def prepare(forward, origins, pieces, vecs_ref):
    side = vecs_ref.shape[-1]
    width, share = pieces[0].shape
    per_piece = share // side
    blocks = len(pieces) * per_piece
    for s, (origin, piece) in enumerate(zip(origins, pieces)):
        for b in range(per_piece):
            x = piece[:, b * side:(b + 1) * side]
            high = x.astype(jnp.bfloat16).astype(jnp.float32)
            rows = [high, x - high]
            if forward:
                rows = jnp.concatenate(rows + [jnp.zeros((side - 2 * width, side), jnp.float32)], axis=0).T
                rows = jnp.concatenate([rows, rows], axis=0)
            else:
                rows = jnp.concatenate(rows, axis=0)
            vecs_ref[origin * per_piece + b] = rows.astype(jnp.bfloat16)
            if s == 0:
                vecs_ref[blocks + b] = (rows * 0.5).astype(jnp.bfloat16)
    vecs_ref[blocks + per_piece] = jnp.zeros_like(vecs_ref[0])


def shifted(steps, n):
    return lax.rem(lax.axis_index("col") + steps % n, n)


def add_products(forward, per_piece, places_ref, count, held_ref, vecs_ref, total_ref):
    side = held_ref.shape[-1]
    blocks = vecs_ref.shape[0] - per_piece - 1
    row_base, col_base = lax.axis_index("row") * per_piece, lax.axis_index("col") * per_piece

    @pl.loop(0, (count + GROUP - 1) // GROUP)
    def _(g):
        for u in range(GROUP):
            t = g * GROUP + u
            i, j = places_ref[0, t], places_ref[1, t]
            diagonal = (i - j == col_base - row_base) & (j >= row_base) & (j < row_base + per_piece)
            source, at, base = (j, i, row_base) if forward else (i, j, col_base)
            source = jnp.where(diagonal, source + (blocks - base), source)
            source = jnp.where(t < count, source, blocks + per_piece)
            high, low = split(held_ref[t])
            both = jnp.concatenate([high, low], axis=1)
            if forward:
                total_ref[at] += jnp.dot(both, vecs_ref[source], preferred_element_type=jnp.float32)
            else:
                out = jnp.dot(vecs_ref[source], both, preferred_element_type=jnp.float32)
                width = out.shape[0] // 2
                total_ref[at] += out[:width, :side] + out[width:, :side] + out[:width, side:]


def forward_kernel(per_piece, list_ref, count_ref, held_ref, *refs):
    *pieces, total_ref, vecs_ref, places_ref, list_sem = refs
    list_copy = pltpu.make_async_copy(list_ref, places_ref, list_sem)
    list_copy.start()
    row_at = lax.axis_index("row")
    prepare(True, [row_at ^ s for s in range(len(pieces))], pieces, vecs_ref)
    total_ref[...] = jnp.zeros_like(total_ref)
    list_copy.wait()
    add_products(True, per_piece, places_ref, count_ref[0, 0], held_ref, vecs_ref, total_ref)


def transposed_kernel(
    per_piece, list_ref, count_ref, held_ref, own_ref, came_ref, _, total_ref, vecs_ref, places_ref, list_sem
):
    list_copy = pltpu.make_async_copy(list_ref, places_ref, list_sem)
    list_copy.start()
    half = own_ref.shape[0]
    origins = [shifted(-2 * q, 2 * half) for q in range(half)]
    prepare(
        False,
        origins + [origin ^ 1 for origin in origins],
        [ref.at[q] for ref in (own_ref, came_ref) for q in range(half)],
        vecs_ref,
    )
    total_ref[...] = jnp.zeros_like(total_ref)
    list_copy.wait()
    add_products(False, per_piece, places_ref, count_ref[0, 0], held_ref, vecs_ref, total_ref)


def route_rows_kernel(total_ref, kept_ref, leaving_ref):
    n = 2 * kept_ref.shape[0]
    per_piece = total_ref.shape[0] // n
    width = kept_ref.shape[1]
    side = total_ref.shape[-1]
    for s in range(n):
        base = (shifted(s // 2 * 2, n) ^ (s % 2)) * per_piece
        out = (leaving_ref if s % 2 else kept_ref).at[s // 2]
        for b in range(per_piece):
            turned = total_ref[base + b].T
            out[:, b * side:(b + 1) * side] = turned[:width] + turned[width:2 * width]


def route_cols_kernel(total_ref, *outs):
    width, share = outs[0].shape
    side = total_ref.shape[-1]
    for s, out in enumerate(outs):
        base = (lax.axis_index("row") ^ s) * (share // side)
        for b in range(share // side):
            out[:, b * side:(b + 1) * side] = total_ref[base + b]


def add_kernel(kept_ref, came_ref, *outs):
    for q, out in enumerate(outs):
        out[...] = kept_ref[q] + came_ref[q]


def sum_kernel(*refs):
    *ins, basis_ref, residual_ref = refs
    vec = basis_ref.shape[0]
    total = ins[0][...]
    for ref in ins[1:]:
        total = total + ref[...]
    basis_ref[...] = total[:vec]
    residual_ref[...] = total[vec:]


def exchange(x, axis, offset):
    return lax.ppermute(x, axis, [(a, a ^ offset) for a in range(lax.axis_size(axis))])


def shift(x, steps):
    n = lax.axis_size("col")
    return lax.ppermute(x, "col", [(a, (a + steps) % n) for a in range(n)])


def local(ham_tiles, tile_list, tile_count, basis_block, residual_block):
    slots, side = ham_tiles.shape[2], ham_tiles.shape[-1]
    vec, share = basis_block.shape
    width = 2 * vec
    per_piece = share // side
    n_row, n_col = lax.axis_size("row"), lax.axis_size("col")
    row_blocks, col_blocks = n_col * per_piece, n_row * per_piece
    tiles = ham_tiles[0, 0]
    listing = tile_list[0, 0].T
    def cost(part):
        return pl.CostEstimate(
            flops=int(part * slots * 2 * side * side * width * 24),
            bytes_accessed=int(part * slots * side * side * 4),
            transcendentals=0,
        )

    stacked = lax.pad(basis_block, 0.0, ((0, vec, 0), (0, 0, 0))) + lax.pad(
        residual_block, 0.0, ((vec, 0, 0), (0, 0, 0))
    )
    own = pl.pallas_call(
        pass_kernel,
        out_shape=f32(width, share),
        in_specs=[VMEM],
        out_specs=VMEM,
        compiler_params=pltpu.CompilerParams(vmem_limit_bytes=2 * MIB),
        cost_estimate=cost(4.0),
        name="own_share",
    )(stacked)
    col_pieces = [own] + [exchange(own, "row", s) for s in range(1, n_row)]
    line = [own] + [shift(own, s) for s in reversed(range(2, n_col, 2))][::-1]
    params = pltpu.CompilerParams(vmem_limit_bytes=16 * MIB)
    total = pl.pallas_call(
        functools.partial(forward_kernel, per_piece),
        out_shape=f32(row_blocks, side, side),
        in_specs=[ANY, SMEM, VMEM] + [VMEM] * n_row,
        out_specs=VMEM,
        scratch_shapes=[
            pltpu.VMEM((col_blocks + per_piece + 1, 2 * side, side), jnp.bfloat16),
            pltpu.SMEM(listing.shape, jnp.int32),
            pltpu.SemaphoreType.DMA(()),
        ],
        compiler_params=params,
        cost_estimate=cost(1.0),
        name="forward_product",
    )(listing, tile_count, tiles, *col_pieces)
    *line, total = lax.optimization_barrier((*line[::-1], total))
    panel = small(gather_kernel, f32(n_col // 2, width, share), "gather_line", *line)
    came = exchange(panel, "col", 1)
    kept, leaving = small(route_rows_kernel, [f32(n_col // 2, width, share)] * 2, "route_rows", total)
    from_core = exchange(leaving, "col", 1)

    piece = f32(width, share)
    line = small(add_kernel, [piece] * (n_col // 2), "add_cores", kept, from_core)
    total = pl.pallas_call(
        functools.partial(transposed_kernel, per_piece),
        out_shape=f32(col_blocks, width, side),
        in_specs=[ANY, SMEM, VMEM, VMEM, VMEM, ANY],
        out_specs=VMEM,
        scratch_shapes=[
            pltpu.VMEM((row_blocks + per_piece + 1, 2 * width, side), jnp.bfloat16),
            pltpu.SMEM(listing.shape, jnp.int32),
            pltpu.SemaphoreType.DMA(()),
        ],
        compiler_params=params,
        cost_estimate=cost(1.0),
        name="transposed_product",
    )(listing, tile_count, tiles, panel, came, line[0])
    lines = [line[0]] + [shift(line[q], 2 * q) for q in range(1, n_col // 2)]
    *lines, total = lax.optimization_barrier((*lines, total))
    away = small(route_cols_kernel, [piece] * n_row, "route_columns", total)
    cols = [away[0]] + [exchange(away[s], "row", s) for s in reversed(range(1, n_row))]
    h_basis, h_residual = small(sum_kernel, [f32(vec, share)] * 2, "sum_pieces", *lines, *cols)
    return (h_basis, h_residual)


def solution(mesh):
    placed = (
        P("row", "col", None, None, None),
        P("row", "col", None, None),
        P("row", "col"),
        P(None, ("row", "col")),
        P(None, ("row", "col")),
    )
    return jax.shard_map(
        local,
        mesh=mesh,
        in_specs=placed,
        out_specs=(P(None, ("row", "col")), P(None, ("row", "col"))),
        check_vma=False,
    )
```

profile of v0, /device:TPU:0, one launch (start us, length us, event | category | flops | bytes accessed | tf_op | source)
XLA Modules:
  0.0 37.3 jit_solution(6036546135558986084)
XLA Ops:
  0.6 0.8 %pad_add_fusion.in_ref = f32[32,512]{1,0:T(8,128)S(1)} fusion(f32[16,512]{1,0:T(8,128)} %param.9, f32[16,512]{1,0:T(8,128)} %param.8), kind=kLoop, calls=%fused_computation | loop fusion | flops 16384 | bytes 131072 | tf_op jit(solution)/shard_map/add | solution.py:189
  1.4 0.0 copy-start
  1.4 0.0 copy-start.1
  1.4 4.0 %collective-permute-start.5 = (f32[32,512]{1,0:T(8,128)S(1)}, f32[32,512]{1,0:T(8,128)S(1)}, u32[]{:S(2)}, u32[]{:S(2)}) collective-permute-start(f32[32,512]{1,0:T(8,128)S(1)} %own_share.1.refs_0_.refs_3_), channel_id=1, source_target_pairs={{0,24},{8,16},{16,8},{24,0},{1,25},{9,17},{17,9},{25,1},{2,26},{10... | collective-permute-start | bytes 196616 | tf_op jit(solution)/shard_map/ppermute | solution.py:165
  5.4 0.5 %collective-permute-start.4 = (f32[32,512]{1,0:T(8,128)S(1)}, f32[32,512]{1,0:T(8,128)S(1)}, u32[]{:S(2)}, u32[]{:S(2)}) collective-permute-start(f32[32,512]{1,0:T(8,128)S(1)} %own_share.1.refs_0_.refs_3_), channel_id=1, source_target_pairs={{0,16},{8,24},{16,0},{24,8},{1,17},{9,25},{17,1},{25,9},{2,18},{10... | collective-permute-start | bytes 196616 | tf_op jit(solution)/shard_map/ppermute | solution.py:165
  5.9 0.1 collective-permute-start.3
  6.0 2.0 %collective-permute-start.2 = (f32[32,512]{1,0:T(8,128)S(1)}, f32[32,512]{1,0:T(8,128)S(1)}, u32[]{:S(2)}, u32[]{:S(2)}) collective-permute-start(f32[32,512]{1,0:T(8,128)S(1)} %own_share.1.refs_0_.refs_3_), channel_id=1, source_target_pairs={{0,2},{1,3},{2,4},{3,5},{4,6},{5,7},{6,0},{7,1},{8,10},{9,11},{10,... | collective-permute-start | bytes 196616 | tf_op jit(solution)/shard_map/ppermute | solution.py:170
  8.0 2.6 %collective-permute-start.1 = (f32[32,512]{1,0:T(8,128)S(1)}, f32[32,512]{1,0:T(8,128)S(1)}, u32[]{:S(2)}, u32[]{:S(2)}) collective-permute-start(f32[32,512]{1,0:T(8,128)S(1)} %own_share.1.refs_0_.refs_3_), channel_id=1, source_target_pairs={{0,4},{1,5},{2,6},{3,7},{4,0},{5,1},{6,2},{7,3},{8,12},{9,13},{10,... | collective-permute-start | bytes 196616 | tf_op jit(solution)/shard_map/ppermute | solution.py:170
  11.3 0.0 collective-permute-done.5.refs_3_
  11.3 1.9 %collective-permute-start = (f32[32,512]{1,0:T(8,128)S(1)}, f32[32,512]{1,0:T(8,128)S(1)}, u32[]{:S(2)}, u32[]{:S(2)}) collective-permute-start(f32[32,512]{1,0:T(8,128)S(1)} %own_share.1.refs_0_.refs_3_), channel_id=1, source_target_pairs={{0,6},{1,7},{2,0},{3,1},{4,2},{5,3},{6,4},{7,5},{8,14},{9,15},{10,... | collective-permute-start | bytes 196616 | tf_op jit(solution)/shard_map/ppermute | solution.py:170
  13.2 0.0 collective-permute-done.4.refs_2_
  13.2 0.0 collective-permute-done.3.refs_1_
  13.2 0.0 copy-done
  13.2 0.0 copy-done.1
  13.2 5.9 %forward_product.1.total_ref = f32[32,128,128]{2,1,0:T(8,128)S(1)} custom-call(s32[2,320]{1,0:T(2,128)S(1)} %bitcast.6, s32[1,1]{1,0:T(1,128)S(6)} %copy.7.count_ref, f32[320,128,128]{2,1,0:T(8,128)S(1)} %bitcast.4, f32[32,512]{1,0:T(8,128)S(1)} %own_share.1.refs_0_.refs_3_, f32[32,512]{1,0:T(8,128)S(1)} %collective-permute-done.3.refs_1_, ...), custom_call_target="tpu_custom_call" | custom-call | flops 8053063680 | bytes 20971520 | tf_op jit(solution)/shard_map/forward_product/pallas_call | solution.py:204
  19.1 0.0 collective-permute-done.2.refs_2_
  19.1 0.0 collective-permute-done.1.refs_1_
  19.1 0.0 collective-permute-done.refs_0_
  19.2 0.6 %route_rows.1 = (f32[4,32,512]{2,1,0:T(8,128)S(1)}, f32[4,32,512]{2,1,0:T(8,128)S(1)}) custom-call(f32[32,128,128]{2,1,0:T(8,128)S(1)} %forward_product.1.total_ref), custom_call_target="tpu_custom_call" | custom-call | tf_op jit(solution)/shard_map/route_rows/pallas_call | solution.py:19
  19.8 0.1 collective-permute-start.6
  19.9 0.6 %collective-permute-start.10 = (f32[4,32,512]{2,1,0:T(8,128)S(1)}, f32[4,32,512]{2,1,0:T(8,128)S(1)}, u32[]{:S(2)}, u32[]{:S(2)}) collective-permute-start(f32[4,32,512]{2,1,0:T(8,128)S(1)} %gather_line.1.own_ref), channel_id=1, source_target_pairs={{0,1},{1,0},{2,3},{3,2},{4,5},{5,4},{6,7},{7,6},{8,9},{9,8},{10,11... | collective-permute-start | bytes 786440 | tf_op jit(solution)/shard_map/ppermute | solution.py:165
  20.4 0.9 %collective-permute-done.6.came_ref = f32[4,32,512]{2,1,0:T(8,128)S(1)} collective-permute-done((f32[4,32,512]{2,1,0:T(8,128)S(1)}, f32[4,32,512]{2,1,0:T(8,128)S(1)}, u32[]{:S(2)}, u32[]{:S(2)}) %collective-permute-start.6) | collective-permute-done | bytes 262176 | tf_op jit(solution)/shard_map/ppermute | solution.py:165
  21.4 0.2 collective-permute-start.7
  21.6 2.4 %collective-permute-start.8 = (f32[32,512]{1,0:T(8,128)S(1)}, f32[32,512]{1,0:T(8,128)S(1)}, u32[]{:S(2)}, u32[]{:S(2)}) collective-permute-start(f32[32,512]{1,0:T(8,128)S(1)} %get-tuple-element.27), channel_id=1, source_target_pairs={{0,4},{1,5},{2,6},{3,7},{4,0},{5,1},{6,2},{7,3},{8,12},{9,13},{10,... | collective-permute-start | bytes 196616 | tf_op jit(solution)/shard_map/ppermute | solution.py:170
  24.0 1.2 %collective-permute-start.9 = (f32[32,512]{1,0:T(8,128)S(1)}, f32[32,512]{1,0:T(8,128)S(1)}, u32[]{:S(2)}, u32[]{:S(2)}) collective-permute-start(f32[32,512]{1,0:T(8,128)S(1)} %get-tuple-element.28), channel_id=1, source_target_pairs={{0,6},{1,7},{2,0},{3,1},{4,2},{5,3},{6,4},{7,5},{8,14},{9,15},{10,... | collective-permute-start | bytes 196616 | tf_op jit(solution)/shard_map/ppermute | solution.py:170
  25.3 0.0 collective-permute-done.10.came_ref
  25.3 3.9 %transposed_product.1.total_ref = f32[16,32,128]{2,1,0:T(8,128)S(1)} custom-call(s32[2,320]{1,0:T(2,128)S(1)} %bitcast.7, s32[1,1]{1,0:T(1,128)S(6)} %copy.7.count_ref, f32[320,128,128]{2,1,0:T(8,128)S(1)} %bitcast.5, f32[4,32,512]{2,1,0:T(8,128)S(1)} %gather_line.1.own_ref, f32[4,32,512]{2,1,0:T(8,128)S(1)} %collective-permute-done.10.came_ref, ...), custom_call_target="tpu_custom_call" | custom-call | flops 8053063680 | bytes 20971520 | tf_op jit(solution)/shard_map/transposed_product/pallas_call | solution.py:226
  29.2 0.0 collective-permute-done.7.refs_1_
  29.2 0.9 %collective-permute-done.8.refs_2_ = f32[32,512]{1,0:T(8,128)S(1)} collective-permute-done((f32[32,512]{1,0:T(8,128)S(1)}, f32[32,512]{1,0:T(8,128)S(1)}, u32[]{:S(2)}, u32[]{:S(2)}) %collective-permute-start.8) | collective-permute-done | bytes 65568 | tf_op jit(solution)/shard_map/ppermute | solution.py:170
  30.1 0.0 collective-permute-done.9.refs_3_
  30.1 0.1 collective-permute-start.11
  30.2 2.2 %collective-permute-start.12 = (f32[32,512]{1,0:T(8,128)S(1)}, f32[32,512]{1,0:T(8,128)S(1)}, u32[]{:S(2)}, u32[]{:S(2)}) collective-permute-start(f32[32,512]{1,0:T(8,128)S(1)} %get-tuple-element.40), channel_id=1, source_target_pairs={{0,16},{8,24},{16,0},{24,8},{1,17},{9,25},{17,1},{25,9},{2,18},{10... | collective-permute-start | bytes 196616 | tf_op jit(solution)/shard_map/ppermute | solution.py:165
  32.4 1.3 %collective-permute-start.13 = (f32[32,512]{1,0:T(8,128)S(1)}, f32[32,512]{1,0:T(8,128)S(1)}, u32[]{:S(2)}, u32[]{:S(2)}) collective-permute-start(f32[32,512]{1,0:T(8,128)S(1)} %get-tuple-element.41), channel_id=1, source_target_pairs={{0,8},{8,0},{16,24},{24,16},{1,9},{9,1},{17,25},{25,17},{2,10},{10... | collective-permute-start | bytes 196616 | tf_op jit(solution)/shard_map/ppermute | solution.py:165
  33.7 1.7 %collective-permute-done.11.refs_5_ = f32[32,512]{1,0:T(8,128)S(1)} collective-permute-done((f32[32,512]{1,0:T(8,128)S(1)}, f32[32,512]{1,0:T(8,128)S(1)}, u32[]{:S(2)}, u32[]{:S(2)}) %collective-permute-start.11) | collective-permute-done | bytes 65568 | tf_op jit(solution)/shard_map/ppermute | solution.py:165
  35.3 0.0 collective-permute-done.12.refs_6_
  35.3 1.3 %collective-permute-done.13.refs_7_ = f32[32,512]{1,0:T(8,128)S(1)} collective-permute-done((f32[32,512]{1,0:T(8,128)S(1)}, f32[32,512]{1,0:T(8,128)S(1)}, u32[]{:S(2)}, u32[]{:S(2)}) %collective-permute-start.13) | collective-permute-done | bytes 65568 | tf_op jit(solution)/shard_map/ppermute | solution.py:165
  36.6 0.6 %sum_pieces.1 = (f32[16,512]{1,0:T(8,128)}, f32[16,512]{1,0:T(8,128)}) custom-call(f32[32,512]{1,0:T(8,128)S(1)} %get-tuple-element.33._.refs_0_, f32[32,512]{1,0:T(8,128)S(1)} %collective-permute-done.7.refs_1_, f32[32,512]{1,0:T(8,128)S(1)} %collective-permute-done.8.refs_2_, f32[32,512]{1,0:T(8,128)S(1)} %collective-permute-done.9.refs_3_, ...), custom_call_target="tpu_custom_call" | custom-call | tf_op jit(solution)/shard_map/sum_pieces/pallas_call | solution.py:19
  (4 shorter events, 0.1 us)
Async XLA Ops:
  1.4 11.8 %copy-start = (f32[1,1,320,128,128]{4,3,2,1,0:T(8,128)S(1)}, f32[1,1,320,128,128]{4,3,2,1,0:T(8,128)}, u32[]{:S(2)}) copy-start(f32[1,1,320,128,128]{4,3,2,1,0:T(8,128)} %param.5) | copy-start | bytes 62914564
  1.4 11.8 %copy-start.1 = (s32[1,1,320,2]{2,3,1,0:T(2,128)S(1)}, s32[1,1,320,2]{2,3,1,0:T(2,128)}, u32[]{:S(2)}) copy-start(s32[1,1,320,2]{2,3,1,0:T(2,128)} %param.6) | copy-start | bytes 7684
  1.4 9.8 %collective-permute-start.5 = (f32[32,512]{1,0:T(8,128)S(1)}, f32[32,512]{1,0:T(8,128)S(1)}, u32[]{:S(2)}, u32[]{:S(2)}) collective-permute-start(f32[32,512]{1,0:T(8,128)S(1)} %own_share.1.refs_0_.refs_3_), channel_id=1, source_target_pairs={{0,24},{8,16},{16,8},{24,0},{1,25},{9,17},{17,9},{25,1},{2,26},{10... | collective-permute-start | bytes 196616 | tf_op jit(solution)/shard_map/ppermute | solution.py:165
  5.4 7.8 %collective-permute-start.4 = (f32[32,512]{1,0:T(8,128)S(1)}, f32[32,512]{1,0:T(8,128)S(1)}, u32[]{:S(2)}, u32[]{:S(2)}) collective-permute-start(f32[32,512]{1,0:T(8,128)S(1)} %own_share.1.refs_0_.refs_3_), channel_id=1, source_target_pairs={{0,16},{8,24},{16,0},{24,8},{1,17},{9,25},{17,1},{25,9},{2,18},{10... | collective-permute-start | bytes 196616 | tf_op jit(solution)/shard_map/ppermute | solution.py:165
  5.9 7.3 %collective-permute-start.3 = (f32[32,512]{1,0:T(8,128)S(1)}, f32[32,512]{1,0:T(8,128)S(1)}, u32[]{:S(2)}, u32[]{:S(2)}) collective-permute-start(f32[32,512]{1,0:T(8,128)S(1)} %own_share.1.refs_0_.refs_3_), channel_id=1, source_target_pairs={{0,8},{8,0},{16,24},{24,16},{1,9},{9,1},{17,25},{25,17},{2,10},{10... | collective-permute-start | bytes 196616 | tf_op jit(solution)/shard_map/ppermute | solution.py:165
  6.0 13.1 %collective-permute-start.2 = (f32[32,512]{1,0:T(8,128)S(1)}, f32[32,512]{1,0:T(8,128)S(1)}, u32[]{:S(2)}, u32[]{:S(2)}) collective-permute-start(f32[32,512]{1,0:T(8,128)S(1)} %own_share.1.refs_0_.refs_3_), channel_id=1, source_target_pairs={{0,2},{1,3},{2,4},{3,5},{4,6},{5,7},{6,0},{7,1},{8,10},{9,11},{10,... | collective-permute-start | bytes 196616 | tf_op jit(solution)/shard_map/ppermute | solution.py:170
  8.0 11.1 %collective-permute-start.1 = (f32[32,512]{1,0:T(8,128)S(1)}, f32[32,512]{1,0:T(8,128)S(1)}, u32[]{:S(2)}, u32[]{:S(2)}) collective-permute-start(f32[32,512]{1,0:T(8,128)S(1)} %own_share.1.refs_0_.refs_3_), channel_id=1, source_target_pairs={{0,4},{1,5},{2,6},{3,7},{4,0},{5,1},{6,2},{7,3},{8,12},{9,13},{10,... | collective-permute-start | bytes 196616 | tf_op jit(solution)/shard_map/ppermute | solution.py:170
  11.3 7.9 %collective-permute-start = (f32[32,512]{1,0:T(8,128)S(1)}, f32[32,512]{1,0:T(8,128)S(1)}, u32[]{:S(2)}, u32[]{:S(2)}) collective-permute-start(f32[32,512]{1,0:T(8,128)S(1)} %own_share.1.refs_0_.refs_3_), channel_id=1, source_target_pairs={{0,6},{1,7},{2,0},{3,1},{4,2},{5,3},{6,4},{7,5},{8,14},{9,15},{10,... | collective-permute-start | bytes 196616 | tf_op jit(solution)/shard_map/ppermute | solution.py:170
  19.8 1.6 %collective-permute-start.6 = (f32[4,32,512]{2,1,0:T(8,128)S(1)}, f32[4,32,512]{2,1,0:T(8,128)S(1)}, u32[]{:S(2)}, u32[]{:S(2)}) collective-permute-start(f32[4,32,512]{2,1,0:T(8,128)S(1)} %get-tuple-element.24), channel_id=1, source_target_pairs={{0,1},{1,0},{2,3},{3,2},{4,5},{5,4},{6,7},{7,6},{8,9},{9,8},{10,11... | collective-permute-start | bytes 786440 | tf_op jit(solution)/shard_map/ppermute | solution.py:165
  19.9 5.4 %collective-permute-start.10 = (f32[4,32,512]{2,1,0:T(8,128)S(1)}, f32[4,32,512]{2,1,0:T(8,128)S(1)}, u32[]{:S(2)}, u32[]{:S(2)}) collective-permute-start(f32[4,32,512]{2,1,0:T(8,128)S(1)} %gather_line.1.own_ref), channel_id=1, source_target_pairs={{0,1},{1,0},{2,3},{3,2},{4,5},{5,4},{6,7},{7,6},{8,9},{9,8},{10,11... | collective-permute-start | bytes 786440 | tf_op jit(solution)/shard_map/ppermute | solution.py:165
  21.4 7.8 %collective-permute-start.7 = (f32[32,512]{1,0:T(8,128)S(1)}, f32[32,512]{1,0:T(8,128)S(1)}, u32[]{:S(2)}, u32[]{:S(2)}) collective-permute-start(f32[32,512]{1,0:T(8,128)S(1)} %get-tuple-element.26), channel_id=1, source_target_pairs={{0,2},{1,3},{2,4},{3,5},{4,6},{5,7},{6,0},{7,1},{8,10},{9,11},{10,... | collective-permute-start | bytes 196616 | tf_op jit(solution)/shard_map/ppermute | solution.py:170
  21.6 8.5 %collective-permute-start.8 = (f32[32,512]{1,0:T(8,128)S(1)}, f32[32,512]{1,0:T(8,128)S(1)}, u32[]{:S(2)}, u32[]{:S(2)}) collective-permute-start(f32[32,512]{1,0:T(8,128)S(1)} %get-tuple-element.27), channel_id=1, source_target_pairs={{0,4},{1,5},{2,6},{3,7},{4,0},{5,1},{6,2},{7,3},{8,12},{9,13},{10,... | collective-permute-start | bytes 196616 | tf_op jit(solution)/shard_map/ppermute | solution.py:170
  24.0 6.1 %collective-permute-start.9 = (f32[32,512]{1,0:T(8,128)S(1)}, f32[32,512]{1,0:T(8,128)S(1)}, u32[]{:S(2)}, u32[]{:S(2)}) collective-permute-start(f32[32,512]{1,0:T(8,128)S(1)} %get-tuple-element.28), channel_id=1, source_target_pairs={{0,6},{1,7},{2,0},{3,1},{4,2},{5,3},{6,4},{7,5},{8,14},{9,15},{10,... | collective-permute-start | bytes 196616 | tf_op jit(solution)/shard_map/ppermute | solution.py:170
  30.1 5.2 %collective-permute-start.11 = (f32[32,512]{1,0:T(8,128)S(1)}, f32[32,512]{1,0:T(8,128)S(1)}, u32[]{:S(2)}, u32[]{:S(2)}) collective-permute-start(f32[32,512]{1,0:T(8,128)S(1)} %get-tuple-element.39), channel_id=1, source_target_pairs={{0,24},{8,16},{16,8},{24,0},{1,25},{9,17},{17,9},{25,1},{2,26},{10... | collective-permute-start | bytes 196616 | tf_op jit(solution)/shard_map/ppermute | solution.py:165
  30.2 5.2 %collective-permute-start.12 = (f32[32,512]{1,0:T(8,128)S(1)}, f32[32,512]{1,0:T(8,128)S(1)}, u32[]{:S(2)}, u32[]{:S(2)}) collective-permute-start(f32[32,512]{1,0:T(8,128)S(1)} %get-tuple-element.40), channel_id=1, source_target_pairs={{0,16},{8,24},{16,0},{24,8},{1,17},{9,25},{17,1},{25,9},{2,18},{10... | collective-permute-start | bytes 196616 | tf_op jit(solution)/shard_map/ppermute | solution.py:165
  32.4 4.3 %collective-permute-start.13 = (f32[32,512]{1,0:T(8,128)S(1)}, f32[32,512]{1,0:T(8,128)S(1)}, u32[]{:S(2)}, u32[]{:S(2)}) collective-permute-start(f32[32,512]{1,0:T(8,128)S(1)} %get-tuple-element.41), channel_id=1, source_target_pairs={{0,8},{8,0},{16,24},{24,16},{1,9},{9,1},{17,25},{25,17},{2,10},{10... | collective-permute-start | bytes 196616 | tf_op jit(solution)/shard_map/ppermute | solution.py:165
where the time goes:
time: 37.5 us; the launch traced here: 37.3 us
  starting transfers between devices  19.1 us (51%)
  Pallas kernels  11.2 us (30%)
  waiting for transfers between devices  4.79 us (13%)
  between operations  1.41 us (4%)
  other arithmetic  0.78 us (2%)
    ppermute x6, starting transfers between devices, shift(): return lax.ppermute(x, 'col', [(a, (a + steps) % n) for a in range(n)])  10.3 us
    ppermute x8, starting transfers between devices, exchange(): lax.ppermute(x, axis, [(a, a ^ offset) for a in range(lax.axis_size(axis))])  8.77 us
    pallas_call x1, Pallas kernels, local(): pl.pallas_call(functools.partial(forward_kernel, per_piece), out_shape=f3...  5.94 us
    pallas_call x1, Pallas kernels, local(): pl.pallas_call(functools.partial(transposed_kernel, per_piece), out_shape...  3.93 us
    ppermute x8, waiting for transfers between devices, exchange(): lax.ppermute(x, axis, [(a, a ^ offset) for a in range(lax.axis_size(axis))])  3.92 us
    pallas_call x5, Pallas kernels, small(): pl.pallas_call(kernel, out_shape=out_shape, in_specs=in_specs or [VMEM] *...  1.31 us
    ppermute x6, waiting for transfers between devices, shift(): return lax.ppermute(x, 'col', [(a, (a + steps) % n) for a in range(n)])  0.88 us
    add x1, other arithmetic, local(): lax.pad(basis_block, 0.0, ((0, vec, 0), (0, 0, 0)))  0.78 us
  transfers between devices with their start and end apart: 14, of which 4 were waited for; matrix products, arithmetic and copies ran while one was open for 0% of the time, Pallas kernels for 27%

commit v1 on v0

--- a/solution.py
+++ b/solution.py
@@ -46,53 +46,46 @@
     return high, low
 
 
-def prepare(forward, origins, pieces, vecs_ref):
+def turned_vectors(x, vecs_ref, at, weight=1.0):
+    width, side = x.shape
+    high = x.astype(jnp.bfloat16).astype(jnp.float32)
+    both = jnp.concatenate([high, x - high] * (side // (2 * width)), axis=0).T * weight
+    column = lax.broadcasted_iota(jnp.int32, both.shape, 1)
+    vecs_ref[0, at] = jnp.where(column < side // 2, both, 0.0).astype(jnp.bfloat16)
+    vecs_ref[1, at] = jnp.where(column < side // 2, 0.0, both).astype(jnp.bfloat16)
+
+
+def plain_vectors(x, vecs_ref, at, weight=1.0):
+    high = x.astype(jnp.bfloat16).astype(jnp.float32)
+    vecs_ref[0, at] = (jnp.concatenate([high, x - high], axis=0) * weight).astype(jnp.bfloat16)
+
+
+def prepare(store, origins, pieces, vecs_ref):
     side = vecs_ref.shape[-1]
-    width, share = pieces[0].shape
-    per_piece = share // side
+    per_piece = pieces[0].shape[1] // side
     blocks = len(pieces) * per_piece
     for s, (origin, piece) in enumerate(zip(origins, pieces)):
         for b in range(per_piece):
             x = piece[:, b * side:(b + 1) * side]
-            high = x.astype(jnp.bfloat16).astype(jnp.float32)
-            rows = [high, x - high]
-            if forward:
-                rows = jnp.concatenate(rows + [jnp.zeros((side - 2 * width, side), jnp.float32)], axis=0).T
-                rows = jnp.concatenate([rows, rows], axis=0)
-            else:
-                rows = jnp.concatenate(rows, axis=0)
-            vecs_ref[origin * per_piece + b] = rows.astype(jnp.bfloat16)
+            store(x, vecs_ref, origin * per_piece + b)
             if s == 0:
-                vecs_ref[blocks + b] = (rows * 0.5).astype(jnp.bfloat16)
-    vecs_ref[blocks + per_piece] = jnp.zeros_like(vecs_ref[0])
+                store(x, vecs_ref, blocks + b, 0.5)
+    for form in range(vecs_ref.shape[0]):
+        vecs_ref[form, blocks + per_piece] = jnp.zeros_like(vecs_ref[0, 0])
 
 
 def shifted(steps, n):
     return lax.rem(lax.axis_index("col") + steps % n, n)
 
 
-def add_products(forward, per_piece, places_ref, count, held_ref, vecs_ref, total_ref):
-    side = held_ref.shape[-1]
-    blocks = vecs_ref.shape[0] - per_piece - 1
+def find_slot(forward, per_piece, t, places_ref, count, vecs_ref):
+    blocks = vecs_ref.shape[1] - per_piece - 1
     row_base, col_base = lax.axis_index("row") * per_piece, lax.axis_index("col") * per_piece
-
-    @pl.loop(0, (count + GROUP - 1) // GROUP)
-    def _(g):
-        for u in range(GROUP):
-            t = g * GROUP + u
-            i, j = places_ref[0, t], places_ref[1, t]
-            diagonal = (i - j == col_base - row_base) & (j >= row_base) & (j < row_base + per_piece)
-            source, at, base = (j, i, row_base) if forward else (i, j, col_base)
-            source = jnp.where(diagonal, source + (blocks - base), source)
-            source = jnp.where(t < count, source, blocks + per_piece)
-            high, low = split(held_ref[t])
-            both = jnp.concatenate([high, low], axis=1)
-            if forward:
-                total_ref[at] += jnp.dot(both, vecs_ref[source], preferred_element_type=jnp.float32)
-            else:
-                out = jnp.dot(vecs_ref[source], both, preferred_element_type=jnp.float32)
-                width = out.shape[0] // 2
-                total_ref[at] += out[:width, :side] + out[width:, :side] + out[:width, side:]
+    i, j = places_ref[0, t], places_ref[1, t]
+    diagonal = (i - j == col_base - row_base) & (j >= row_base) & (j < row_base + per_piece)
+    source, at, base = (j, i, row_base) if forward else (i, j, col_base)
+    source = jnp.where(diagonal, source + (blocks - base), source)
+    return jnp.where(t < count, source, blocks + per_piece), at
 
 
 def forward_kernel(per_piece, list_ref, count_ref, held_ref, *refs):
@@ -100,10 +93,33 @@
     list_copy = pltpu.make_async_copy(list_ref, places_ref, list_sem)
     list_copy.start()
     row_at = lax.axis_index("row")
-    prepare(True, [row_at ^ s for s in range(len(pieces))], pieces, vecs_ref)
+    prepare(turned_vectors, [row_at ^ s for s in range(len(pieces))], pieces, vecs_ref)
     total_ref[...] = jnp.zeros_like(total_ref)
     list_copy.wait()
-    add_products(True, per_piece, places_ref, count_ref[0, 0], held_ref, vecs_ref, total_ref)
+    count = count_ref[0, 0]
+    side = held_ref.shape[-1]
+    step = 16
+
+    @pl.loop(0, (count + GROUP - 1) // GROUP)
+    def _(g):
+        for u in range(0, GROUP, 2):
+            slots = [g * GROUP + u + h for h in range(2)]
+            found = [find_slot(True, per_piece, t, places_ref, count, vecs_ref) for t in slots]
+            rows = []
+            for t in slots:
+                high, low = split(held_ref[t])
+                for r in range(0, side, step):
+                    rows += [high[r:r + step], low[r:r + step]]
+            out = jnp.dot(
+                jnp.concatenate(rows, axis=0),
+                vecs_ref[0, found[0][0]] + vecs_ref[1, found[1][0]],
+                preferred_element_type=jnp.float32,
+            )
+            for h in range(2):
+                at = found[h][1]
+                for r in range(0, side, step):
+                    lies = 2 * (side * h + r)
+                    total_ref[h, at, r:r + step] += out[lies:lies + step] + out[lies + step:lies + 2 * step]
 
 
 def transposed_kernel(
@@ -114,27 +130,43 @@
     half = own_ref.shape[0]
     origins = [shifted(-2 * q, 2 * half) for q in range(half)]
     prepare(
-        False,
+        plain_vectors,
         origins + [origin ^ 1 for origin in origins],
         [ref.at[q] for ref in (own_ref, came_ref) for q in range(half)],
         vecs_ref,
     )
     total_ref[...] = jnp.zeros_like(total_ref)
     list_copy.wait()
-    add_products(False, per_piece, places_ref, count_ref[0, 0], held_ref, vecs_ref, total_ref)
-
-
-def route_rows_kernel(total_ref, kept_ref, leaving_ref):
-    n = 2 * kept_ref.shape[0]
-    per_piece = total_ref.shape[0] // n
-    width = kept_ref.shape[1]
+    count = count_ref[0, 0]
+    width, side = total_ref.shape[1:]
+
+    @pl.loop(0, (count + GROUP - 1) // GROUP)
+    def _(g):
+        for u in range(GROUP):
+            t = g * GROUP + u
+            source, at = find_slot(False, per_piece, t, places_ref, count, vecs_ref)
+            out = jnp.dot(
+                vecs_ref[0, source],
+                jnp.concatenate(split(held_ref[t]), axis=1),
+                preferred_element_type=jnp.float32,
+            )
+            total_ref[at] += out[:width, :side] + out[width:, :side] + out[:width, side:]
+
+
+def route_rows_kernel(other, total_ref, out_ref):
+    n = 2 * out_ref.shape[0]
+    per_piece = total_ref.shape[1] // n
+    width = out_ref.shape[1]
     side = total_ref.shape[-1]
-    for s in range(n):
-        base = (shifted(s // 2 * 2, n) ^ (s % 2)) * per_piece
-        out = (leaving_ref if s % 2 else kept_ref).at[s // 2]
+    column = lax.broadcasted_iota(jnp.int32, (side, side), 1)
+    for q in range(n // 2):
+        base = (shifted(2 * q, n) ^ other) * per_piece
         for b in range(per_piece):
-            turned = total_ref[base + b].T
-            out[:, b * side:(b + 1) * side] = turned[:width] + turned[width:2 * width]
+            turned = jnp.where(column < side // 2, total_ref[0, base + b], total_ref[1, base + b]).T
+            block = turned[:width]
+            for v in range(width, side, width):
+                block = block + turned[v:v + width]
+            out_ref[q, :, b * side:(b + 1) * side] = block
 
 
 def route_cols_kernel(total_ref, *outs):
@@ -203,11 +235,11 @@
     params = pltpu.CompilerParams(vmem_limit_bytes=16 * MIB)
     total = pl.pallas_call(
         functools.partial(forward_kernel, per_piece),
-        out_shape=f32(row_blocks, side, side),
+        out_shape=f32(2, row_blocks, side, side),
         in_specs=[ANY, SMEM, VMEM] + [VMEM] * n_row,
         out_specs=VMEM,
         scratch_shapes=[
-            pltpu.VMEM((col_blocks + per_piece + 1, 2 * side, side), jnp.bfloat16),
+            pltpu.VMEM((2, col_blocks + per_piece + 1, side, side), jnp.bfloat16),
             pltpu.SMEM(listing.shape, jnp.int32),
             pltpu.SemaphoreType.DMA(()),
         ],
@@ -218,9 +250,11 @@
     *line, total = lax.optimization_barrier((*line[::-1], total))
     panel = small(gather_kernel, f32(n_col // 2, width, share), "gather_line", *line)
     came = exchange(panel, "col", 1)
-    kept, leaving = small(route_rows_kernel, [f32(n_col // 2, width, share)] * 2, "route_rows", total)
+    pieces = f32(n_col // 2, width, share)
+    leaving = small(functools.partial(route_rows_kernel, 1), pieces, "route_leaving", total)
     from_core = exchange(leaving, "col", 1)
-
+    leaving, total = lax.optimization_barrier((leaving, total))
+    kept = small(functools.partial(route_rows_kernel, 0), pieces, "route_kept", total)
     piece = f32(width, share)
     line = small(add_kernel, [piece] * (n_col // 2), "add_cores", kept, from_core)
     total = pl.pallas_call(
@@ -229,7 +263,7 @@
         in_specs=[ANY, SMEM, VMEM, VMEM, VMEM, ANY],
         out_specs=VMEM,
         scratch_shapes=[
-            pltpu.VMEM((row_blocks + per_piece + 1, 2 * width, side), jnp.bfloat16),
+            pltpu.VMEM((1, row_blocks + per_piece + 1, 2 * width, side), jnp.bfloat16),
             pltpu.SMEM(listing.shape, jnp.int32),
             pltpu.SemaphoreType.DMA(()),
         ],

time: 37.5 us -> 36.4 us (0.971)
  Pallas kernels: 11.2 us -> 9.99 us
    pallas_call x1, Pallas kernels: 5.94 us -> 5.18 us  [local(): pl.pallas_call(functools.partial(forward_kernel, per_piece), out_shape=f3...]
    ppermute x6, waiting for transfers between devices: 0.88 us -> 1.45 us  [shift(): return lax.ppermute(x, 'col', [(a, (a + steps) % n) for a in range(n)])]
    pallas_call x1, Pallas kernels: 3.93 us -> 3.41 us  [local(): pl.pallas_call(functools.partial(transposed_kernel, per_piece), out_shape...]
    ppermute x8, waiting for transfers between devices: 3.92 us -> 3.42 us  [exchange(): lax.ppermute(x, axis, [(a, a ^ offset) for a in range(lax.axis_size(axis))])]
    pallas_call x5 -> x6, Pallas kernels: 1.31 us -> 1.4 us  [small(): pl.pallas_call(kernel, out_shape=out_shape, in_specs=in_specs or [VMEM] *...]
  transfers between devices with their start and end apart: 14 -> 14, of which waited for: 4 -> 4; matrix products, arithmetic and copies ran while one was open for 0% -> 0% of each run, Pallas kernels for 27% -> 25%
where the time goes in v1:
time: 36.4 us; the launch traced here: 36.3 us
  starting transfers between devices  19.2 us (53%)
  Pallas kernels  9.99 us (27%)
  waiting for transfers between devices  4.87 us (13%)
  between operations  1.41 us (4%)
  other arithmetic  0.78 us (2%)
    ppermute x6, starting transfers between devices, shift(): return lax.ppermute(x, 'col', [(a, (a + steps) % n) for a in range(n)])  10.4 us
    ppermute x8, starting transfers between devices, exchange(): lax.ppermute(x, axis, [(a, a ^ offset) for a in range(lax.axis_size(axis))])  8.78 us
    pallas_call x1, Pallas kernels, local(): pl.pallas_call(functools.partial(forward_kernel, per_piece), out_shape=f3...  5.18 us
    ppermute x8, waiting for transfers between devices, exchange(): lax.ppermute(x, axis, [(a, a ^ offset) for a in range(lax.axis_size(axis))])  3.42 us
    pallas_call x1, Pallas kernels, local(): pl.pallas_call(functools.partial(transposed_kernel, per_piece), out_shape...  3.41 us
    ppermute x6, waiting for transfers between devices, shift(): return lax.ppermute(x, 'col', [(a, (a + steps) % n) for a in range(n)])  1.45 us
    pallas_call x6, Pallas kernels, small(): pl.pallas_call(kernel, out_shape=out_shape, in_specs=in_specs or [VMEM] *...  1.4 us
    add x1, other arithmetic, local(): lax.pad(basis_block, 0.0, ((0, vec, 0), (0, 0, 0)))  0.78 us
  transfers between devices with their start and end apart: 14, of which 4 were waited for; matrix products, arithmetic and copies ran while one was open for 0% of the time, Pallas kernels for 25%

profile of v1, /device:TPU:0, one launch (start us, length us, event | category | flops | bytes accessed | tf_op | source)
XLA Modules:
  0.0 36.3 jit_solution(5160368636554487331)
XLA Ops:
  0.6 0.8 %pad_add_fusion.in_ref = f32[32,512]{1,0:T(8,128)S(1)} fusion(f32[16,512]{1,0:T(8,128)} %param.9, f32[16,512]{1,0:T(8,128)} %param.8), kind=kLoop, calls=%fused_computation | loop fusion | flops 16384 | bytes 131072 | tf_op jit(solution)/shard_map/add | solution.py:221
  1.4 0.0 copy-start
  1.4 0.0 copy-start.1
  1.4 4.0 %collective-permute-start.5 = (f32[32,512]{1,0:T(8,128)S(1)}, f32[32,512]{1,0:T(8,128)S(1)}, u32[]{:S(2)}, u32[]{:S(2)}) collective-permute-start(f32[32,512]{1,0:T(8,128)S(1)} %own_share.1.refs_0_.refs_3_), channel_id=1, source_target_pairs={{0,24},{8,16},{16,8},{24,0},{1,25},{9,17},{17,9},{25,1},{2,26},{10... | collective-permute-start | bytes 196616 | tf_op jit(solution)/shard_map/ppermute | solution.py:197
  5.4 0.5 %collective-permute-start.4 = (f32[32,512]{1,0:T(8,128)S(1)}, f32[32,512]{1,0:T(8,128)S(1)}, u32[]{:S(2)}, u32[]{:S(2)}) collective-permute-start(f32[32,512]{1,0:T(8,128)S(1)} %own_share.1.refs_0_.refs_3_), channel_id=1, source_target_pairs={{0,16},{8,24},{16,0},{24,8},{1,17},{9,25},{17,1},{25,9},{2,18},{10... | collective-permute-start | bytes 196616 | tf_op jit(solution)/shard_map/ppermute | solution.py:197
  5.9 0.1 collective-permute-start.3
  6.0 2.0 %collective-permute-start.2 = (f32[32,512]{1,0:T(8,128)S(1)}, f32[32,512]{1,0:T(8,128)S(1)}, u32[]{:S(2)}, u32[]{:S(2)}) collective-permute-start(f32[32,512]{1,0:T(8,128)S(1)} %own_share.1.refs_0_.refs_3_), channel_id=1, source_target_pairs={{0,2},{1,3},{2,4},{3,5},{4,6},{5,7},{6,0},{7,1},{8,10},{9,11},{10,... | collective-permute-start | bytes 196616 | tf_op jit(solution)/shard_map/ppermute | solution.py:202
  8.0 2.6 %collective-permute-start.1 = (f32[32,512]{1,0:T(8,128)S(1)}, f32[32,512]{1,0:T(8,128)S(1)}, u32[]{:S(2)}, u32[]{:S(2)}) collective-permute-start(f32[32,512]{1,0:T(8,128)S(1)} %own_share.1.refs_0_.refs_3_), channel_id=1, source_target_pairs={{0,4},{1,5},{2,6},{3,7},{4,0},{5,1},{6,2},{7,3},{8,12},{9,13},{10,... | collective-permute-start | bytes 196616 | tf_op jit(solution)/shard_map/ppermute | solution.py:202
  11.3 0.0 collective-permute-done.5.refs_3_
  11.3 1.9 %collective-permute-start = (f32[32,512]{1,0:T(8,128)S(1)}, f32[32,512]{1,0:T(8,128)S(1)}, u32[]{:S(2)}, u32[]{:S(2)}) collective-permute-start(f32[32,512]{1,0:T(8,128)S(1)} %own_share.1.refs_0_.refs_3_), channel_id=1, source_target_pairs={{0,6},{1,7},{2,0},{3,1},{4,2},{5,3},{6,4},{7,5},{8,14},{9,15},{10,... | collective-permute-start | bytes 196616 | tf_op jit(solution)/shard_map/ppermute | solution.py:202
  13.2 0.0 collective-permute-done.4.refs_2_
  13.2 0.0 collective-permute-done.3.refs_1_
  13.2 0.0 copy-done
  13.2 0.0 copy-done.1
  13.2 5.2 %forward_product.1.total_ref = f32[2,32,128,128]{3,2,1,0:T(8,128)S(1)} custom-call(s32[2,320]{1,0:T(2,128)S(1)} %bitcast.6, s32[1,1]{1,0:T(1,128)S(6)} %copy.7.count_ref, f32[320,128,128]{2,1,0:T(8,128)S(1)} %bitcast.4, f32[32,512]{1,0:T(8,128)S(1)} %own_share.1.refs_0_.refs_3_, f32[32,512]{1,0:T(8,128)S(1)} %collective-permute-done.3.refs_1_, ...), custom_call_target="tpu_custom_call" | custom-call | flops 8053063680 | bytes 20971520 | tf_op jit(solution)/shard_map/forward_product/pallas_call | solution.py:236
  18.4 0.0 collective-permute-done.2.refs_2_
  18.4 0.0 collective-permute-done.1.refs_1_
  18.4 0.0 collective-permute-done.refs_0_
  18.4 0.3 route_leaving.1
  18.8 0.1 collective-permute-start.6
  18.9 0.6 %collective-permute-start.10 = (f32[4,32,512]{2,1,0:T(8,128)S(1)}, f32[4,32,512]{2,1,0:T(8,128)S(1)}, u32[]{:S(2)}, u32[]{:S(2)}) collective-permute-start(f32[4,32,512]{2,1,0:T(8,128)S(1)} %gather_line.1.own_ref), channel_id=1, source_target_pairs={{0,1},{1,0},{2,3},{3,2},{4,5},{5,4},{6,7},{7,6},{8,9},{9,8},{10,11... | collective-permute-start | bytes 786440 | tf_op jit(solution)/shard_map/ppermute | solution.py:197
  19.4 0.3 route_kept.1.kept_ref
  19.8 0.6 %collective-permute-done.6.came_ref = f32[4,32,512]{2,1,0:T(8,128)S(1)} collective-permute-done((f32[4,32,512]{2,1,0:T(8,128)S(1)}, f32[4,32,512]{2,1,0:T(8,128)S(1)}, u32[]{:S(2)}, u32[]{:S(2)}) %collective-permute-start.6) | collective-permute-done | bytes 262176 | tf_op jit(solution)/shard_map/ppermute | solution.py:197
  20.4 0.3 collective-permute-start.7
  20.7 3.2 %collective-permute-start.8 = (f32[32,512]{1,0:T(8,128)S(1)}, f32[32,512]{1,0:T(8,128)S(1)}, u32[]{:S(2)}, u32[]{:S(2)}) collective-permute-start(f32[32,512]{1,0:T(8,128)S(1)} %get-tuple-element.25), channel_id=1, source_target_pairs={{0,4},{1,5},{2,6},{3,7},{4,0},{5,1},{6,2},{7,3},{8,12},{9,13},{10,... | collective-permute-start | bytes 196616 | tf_op jit(solution)/shard_map/ppermute | solution.py:202
  23.9 0.5 %collective-permute-start.9 = (f32[32,512]{1,0:T(8,128)S(1)}, f32[32,512]{1,0:T(8,128)S(1)}, u32[]{:S(2)}, u32[]{:S(2)}) collective-permute-start(f32[32,512]{1,0:T(8,128)S(1)} %get-tuple-element.26), channel_id=1, source_target_pairs={{0,6},{1,7},{2,0},{3,1},{4,2},{5,3},{6,4},{7,5},{8,14},{9,15},{10,... | collective-permute-start | bytes 196616 | tf_op jit(solution)/shard_map/ppermute | solution.py:202
  24.4 0.0 collective-permute-done.10.came_ref
  24.4 3.4 %transposed_product.1.total_ref = f32[16,32,128]{2,1,0:T(8,128)S(1)} custom-call(s32[2,320]{1,0:T(2,128)S(1)} %bitcast.7, s32[1,1]{1,0:T(1,128)S(6)} %copy.7.count_ref, f32[320,128,128]{2,1,0:T(8,128)S(1)} %bitcast.5, f32[4,32,512]{2,1,0:T(8,128)S(1)} %gather_line.1.own_ref, f32[4,32,512]{2,1,0:T(8,128)S(1)} %collective-permute-done.10.came_ref, ...), custom_call_target="tpu_custom_call" | custom-call | flops 8053063680 | bytes 20971520 | tf_op jit(solution)/shard_map/transposed_product/pallas_call | solution.py:260
  27.8 0.0 collective-permute-done.7.refs_1_
  27.8 1.4 %collective-permute-done.8.refs_2_ = f32[32,512]{1,0:T(8,128)S(1)} collective-permute-done((f32[32,512]{1,0:T(8,128)S(1)}, f32[32,512]{1,0:T(8,128)S(1)}, u32[]{:S(2)}, u32[]{:S(2)}) %collective-permute-start.8) | collective-permute-done | bytes 65568 | tf_op jit(solution)/shard_map/ppermute | solution.py:202
  29.2 0.0 collective-permute-done.9.refs_3_
  29.3 0.2 collective-permute-start.11
  29.5 1.9 %collective-permute-start.12 = (f32[32,512]{1,0:T(8,128)S(1)}, f32[32,512]{1,0:T(8,128)S(1)}, u32[]{:S(2)}, u32[]{:S(2)}) collective-permute-start(f32[32,512]{1,0:T(8,128)S(1)} %get-tuple-element.38), channel_id=1, source_target_pairs={{0,16},{8,24},{16,0},{24,8},{1,17},{9,25},{17,1},{25,9},{2,18},{10... | collective-permute-start | bytes 196616 | tf_op jit(solution)/shard_map/ppermute | solution.py:197
  31.4 1.4 %collective-permute-start.13 = (f32[32,512]{1,0:T(8,128)S(1)}, f32[32,512]{1,0:T(8,128)S(1)}, u32[]{:S(2)}, u32[]{:S(2)}) collective-permute-start(f32[32,512]{1,0:T(8,128)S(1)} %get-tuple-element.39), channel_id=1, source_target_pairs={{0,8},{8,0},{16,24},{24,16},{1,9},{9,1},{17,25},{25,17},{2,10},{10... | collective-permute-start | bytes 196616 | tf_op jit(solution)/shard_map/ppermute | solution.py:197
  32.8 1.7 %collective-permute-done.11.refs_5_ = f32[32,512]{1,0:T(8,128)S(1)} collective-permute-done((f32[32,512]{1,0:T(8,128)S(1)}, f32[32,512]{1,0:T(8,128)S(1)}, u32[]{:S(2)}, u32[]{:S(2)}) %collective-permute-start.11) | collective-permute-done | bytes 65568 | tf_op jit(solution)/shard_map/ppermute | solution.py:197
  34.5 0.0 collective-permute-done.12.refs_6_
  34.5 1.1 %collective-permute-done.13.refs_7_ = f32[32,512]{1,0:T(8,128)S(1)} collective-permute-done((f32[32,512]{1,0:T(8,128)S(1)}, f32[32,512]{1,0:T(8,128)S(1)}, u32[]{:S(2)}, u32[]{:S(2)}) %collective-permute-start.13) | collective-permute-done | bytes 65568 | tf_op jit(solution)/shard_map/ppermute | solution.py:197
  35.6 0.6 %sum_pieces.1 = (f32[16,512]{1,0:T(8,128)}, f32[16,512]{1,0:T(8,128)}) custom-call(f32[32,512]{1,0:T(8,128)S(1)} %get-tuple-element.31._.refs_0_, f32[32,512]{1,0:T(8,128)S(1)} %collective-permute-done.7.refs_1_, f32[32,512]{1,0:T(8,128)S(1)} %collective-permute-done.8.refs_2_, f32[32,512]{1,0:T(8,128)S(1)} %collective-permute-done.9.refs_3_, ...), custom_call_target="tpu_custom_call" | custom-call | tf_op jit(solution)/shard_map/sum_pieces/pallas_call | solution.py:19
  (4 shorter events, 0.1 us)
Async XLA Ops:
  1.4 11.8 %copy-start = (f32[1,1,320,128,128]{4,3,2,1,0:T(8,128)S(1)}, f32[1,1,320,128,128]{4,3,2,1,0:T(8,128)}, u32[]{:S(2)}) copy-start(f32[1,1,320,128,128]{4,3,2,1,0:T(8,128)} %param.5) | copy-start | bytes 62914564
  1.4 11.8 %copy-start.1 = (s32[1,1,320,2]{2,3,1,0:T(2,128)S(1)}, s32[1,1,320,2]{2,3,1,0:T(2,128)}, u32[]{:S(2)}) copy-start(s32[1,1,320,2]{2,3,1,0:T(2,128)} %param.6) | copy-start | bytes 7684
  1.4 9.8 %collective-permute-start.5 = (f32[32,512]{1,0:T(8,128)S(1)}, f32[32,512]{1,0:T(8,128)S(1)}, u32[]{:S(2)}, u32[]{:S(2)}) collective-permute-start(f32[32,512]{1,0:T(8,128)S(1)} %own_share.1.refs_0_.refs_3_), channel_id=1, source_target_pairs={{0,24},{8,16},{16,8},{24,0},{1,25},{9,17},{17,9},{25,1},{2,26},{10... | collective-permute-start | bytes 196616 | tf_op jit(solution)/shard_map/ppermute | solution.py:197
  5.4 7.8 %collective-permute-start.4 = (f32[32,512]{1,0:T(8,128)S(1)}, f32[32,512]{1,0:T(8,128)S(1)}, u32[]{:S(2)}, u32[]{:S(2)}) collective-permute-start(f32[32,512]{1,0:T(8,128)S(1)} %own_share.1.refs_0_.refs_3_), channel_id=1, source_target_pairs={{0,16},{8,24},{16,0},{24,8},{1,17},{9,25},{17,1},{25,9},{2,18},{10... | collective-permute-start | bytes 196616 | tf_op jit(solution)/shard_map/ppermute | solution.py:197
  5.9 7.3 %collective-permute-start.3 = (f32[32,512]{1,0:T(8,128)S(1)}, f32[32,512]{1,0:T(8,128)S(1)}, u32[]{:S(2)}, u32[]{:S(2)}) collective-permute-start(f32[32,512]{1,0:T(8,128)S(1)} %own_share.1.refs_0_.refs_3_), channel_id=1, source_target_pairs={{0,8},{8,0},{16,24},{24,16},{1,9},{9,1},{17,25},{25,17},{2,10},{10... | collective-permute-start | bytes 196616 | tf_op jit(solution)/shard_map/ppermute | solution.py:197
  6.0 12.3 %collective-permute-start.2 = (f32[32,512]{1,0:T(8,128)S(1)}, f32[32,512]{1,0:T(8,128)S(1)}, u32[]{:S(2)}, u32[]{:S(2)}) collective-permute-start(f32[32,512]{1,0:T(8,128)S(1)} %own_share.1.refs_0_.refs_3_), channel_id=1, source_target_pairs={{0,2},{1,3},{2,4},{3,5},{4,6},{5,7},{6,0},{7,1},{8,10},{9,11},{10,... | collective-permute-start | bytes 196616 | tf_op jit(solution)/shard_map/ppermute | solution.py:202
  8.0 10.4 %collective-permute-start.1 = (f32[32,512]{1,0:T(8,128)S(1)}, f32[32,512]{1,0:T(8,128)S(1)}, u32[]{:S(2)}, u32[]{:S(2)}) collective-permute-start(f32[32,512]{1,0:T(8,128)S(1)} %own_share.1.refs_0_.refs_3_), channel_id=1, source_target_pairs={{0,4},{1,5},{2,6},{3,7},{4,0},{5,1},{6,2},{7,3},{8,12},{9,13},{10,... | collective-permute-start | bytes 196616 | tf_op jit(solution)/shard_map/ppermute | solution.py:202
  11.3 7.1 %collective-permute-start = (f32[32,512]{1,0:T(8,128)S(1)}, f32[32,512]{1,0:T(8,128)S(1)}, u32[]{:S(2)}, u32[]{:S(2)}) collective-permute-start(f32[32,512]{1,0:T(8,128)S(1)} %own_share.1.refs_0_.refs_3_), channel_id=1, source_target_pairs={{0,6},{1,7},{2,0},{3,1},{4,2},{5,3},{6,4},{7,5},{8,14},{9,15},{10,... | collective-permute-start | bytes 196616 | tf_op jit(solution)/shard_map/ppermute | solution.py:202
  18.8 1.6 %collective-permute-start.6 = (f32[4,32,512]{2,1,0:T(8,128)S(1)}, f32[4,32,512]{2,1,0:T(8,128)S(1)}, u32[]{:S(2)}, u32[]{:S(2)}) collective-permute-start(f32[4,32,512]{2,1,0:T(8,128)S(1)} %route_leaving.1), channel_id=1, source_target_pairs={{0,1},{1,0},{2,3},{3,2},{4,5},{5,4},{6,7},{7,6},{8,9},{9,8},{10,11... | collective-permute-start | bytes 786440 | tf_op jit(solution)/shard_map/ppermute | solution.py:197
  18.9 5.5 %collective-permute-start.10 = (f32[4,32,512]{2,1,0:T(8,128)S(1)}, f32[4,32,512]{2,1,0:T(8,128)S(1)}, u32[]{:S(2)}, u32[]{:S(2)}) collective-permute-start(f32[4,32,512]{2,1,0:T(8,128)S(1)} %gather_line.1.own_ref), channel_id=1, source_target_pairs={{0,1},{1,0},{2,3},{3,2},{4,5},{5,4},{6,7},{7,6},{8,9},{9,8},{10,11... | collective-permute-start | bytes 786440 | tf_op jit(solution)/shard_map/ppermute | solution.py:197
  20.4 7.4 %collective-permute-start.7 = (f32[32,512]{1,0:T(8,128)S(1)}, f32[32,512]{1,0:T(8,128)S(1)}, u32[]{:S(2)}, u32[]{:S(2)}) collective-permute-start(f32[32,512]{1,0:T(8,128)S(1)} %get-tuple-element.24), channel_id=1, source_target_pairs={{0,2},{1,3},{2,4},{3,5},{4,6},{5,7},{6,0},{7,1},{8,10},{9,11},{10,... | collective-permute-start | bytes 196616 | tf_op jit(solution)/shard_map/ppermute | solution.py:202
  20.7 8.5 %collective-permute-start.8 = (f32[32,512]{1,0:T(8,128)S(1)}, f32[32,512]{1,0:T(8,128)S(1)}, u32[]{:S(2)}, u32[]{:S(2)}) collective-permute-start(f32[32,512]{1,0:T(8,128)S(1)} %get-tuple-element.25), channel_id=1, source_target_pairs={{0,4},{1,5},{2,6},{3,7},{4,0},{5,1},{6,2},{7,3},{8,12},{9,13},{10,... | collective-permute-start | bytes 196616 | tf_op jit(solution)/shard_map/ppermute | solution.py:202
  23.9 5.4 %collective-permute-start.9 = (f32[32,512]{1,0:T(8,128)S(1)}, f32[32,512]{1,0:T(8,128)S(1)}, u32[]{:S(2)}, u32[]{:S(2)}) collective-permute-start(f32[32,512]{1,0:T(8,128)S(1)} %get-tuple-element.26), channel_id=1, source_target_pairs={{0,6},{1,7},{2,0},{3,1},{4,2},{5,3},{6,4},{7,5},{8,14},{9,15},{10,... | collective-permute-start | bytes 196616 | tf_op jit(solution)/shard_map/ppermute | solution.py:202
  29.3 5.2 %collective-permute-start.11 = (f32[32,512]{1,0:T(8,128)S(1)}, f32[32,512]{1,0:T(8,128)S(1)}, u32[]{:S(2)}, u32[]{:S(2)}) collective-permute-start(f32[32,512]{1,0:T(8,128)S(1)} %get-tuple-element.37), channel_id=1, source_target_pairs={{0,24},{8,16},{16,8},{24,0},{1,25},{9,17},{17,9},{25,1},{2,26},{10... | collective-permute-start | bytes 196616 | tf_op jit(solution)/shard_map/ppermute | solution.py:197
  29.5 5.0 %collective-permute-start.12 = (f32[32,512]{1,0:T(8,128)S(1)}, f32[32,512]{1,0:T(8,128)S(1)}, u32[]{:S(2)}, u32[]{:S(2)}) collective-permute-start(f32[32,512]{1,0:T(8,128)S(1)} %get-tuple-element.38), channel_id=1, source_target_pairs={{0,16},{8,24},{16,0},{24,8},{1,17},{9,25},{17,1},{25,9},{2,18},{10... | collective-permute-start | bytes 196616 | tf_op jit(solution)/shard_map/ppermute | solution.py:197
  31.4 4.3 %collective-permute-start.13 = (f32[32,512]{1,0:T(8,128)S(1)}, f32[32,512]{1,0:T(8,128)S(1)}, u32[]{:S(2)}, u32[]{:S(2)}) collective-permute-start(f32[32,512]{1,0:T(8,128)S(1)} %get-tuple-element.39), channel_id=1, source_target_pairs={{0,8},{8,0},{16,24},{24,16},{1,9},{9,1},{17,25},{25,17},{2,10},{10... | collective-permute-start | bytes 196616 | tf_op jit(solution)/shard_map/ppermute | solution.py:197
